TPU v7x, 512 devices: a whole 4x8x8 slice. The times are simulated.
512 devices in a mesh: dp: 8 (over z), fsdp: 64 (over x, y, core).
Axes of the slice: x: 4, y: 8, z: 8, core: 2. Of those that a mesh axis runs over, the one named last changes fastest.
Arguments:
- grad_parts: bfloat16 [8, 224, 512, 512], P('dp', None, 'fsdp'), may hold values from -4 to 4
- owner_map: int32 [224], replicated, may hold values from 0 to 63, as said below
- apply_map: int32 [224, 2], replicated, may hold values from 0 to 63, as said below
- gram_old: bfloat16 [8, 64, 2, 512, 512], P('dp', 'fsdp'), may hold values from -59.73638 to 919.89638, as said below
- old_vectors: bfloat16 [8, 64, 2, 512, 512], P('dp', 'fsdp'), may hold values from -1 to 1
Outputs:
- eig_codes: bfloat16 [8, 64, 2, 512, 512], P('dp', 'fsdp')
- eig_scales: bfloat16 [8, 64, 2, 512, 8], P('dp', 'fsdp')
Inputs may be any that keep to these rules, and one draw needn't show every extreme that they name: `owner_map`: within one dp index (blocks e * 28 to e * 28 + 27) no two blocks share an owner, and of the fsdp indices f and f + 32 at most one owns a block of it. `apply_map`: within one dp index each fsdp index receives at most 2 of the 56 factors, and some fsdp index receives exactly 2 in every dp index. `gram_old`: each [512, 512] matrix is symmetric.
All inputs are finite; a program needn't handle non-finite values. Where the computation divides by a largest or mean magnitude, that divisor is 1e-20 or more.
Results may differ from a plain program's by a relative error of at most 0.017.
Values may be sent and summed in bfloat16 or wider, within the bound.
A program may use at most 64 MiB of HBM per device.

v0:
```python
import jax
import jax.numpy as jnp
from jax import lax
from jax.sharding import PartitionSpec as P

QG = 64
ITERS = 2
AP_CAP = 2


ema_decay = 0.95
norm_eps = 1e-06


def quantize(iterate):
    extent = iterate.shape[0]
    grouped = iterate.reshape(extent, extent // QG, QG)
    group_scale = (jnp.max(jnp.abs(grouped), axis=2) + norm_eps).astype(jnp.bfloat16)
    code_tiles = (grouped / group_scale.astype(jnp.float32)[:, :, None]).astype(jnp.bfloat16)
    return (code_tiles.reshape(extent, extent), group_scale)


def refresh(side_matrix, old_state, old_basis):
    gram_sum = jnp.dot(side_matrix, side_matrix.T, preferred_element_type=jnp.float32)
    ema_state = ema_decay * old_state.astype(jnp.float32) + (1.0 - ema_decay) * gram_sum
    projected = jnp.dot(ema_state, old_basis.astype(jnp.float32), precision=lax.Precision.HIGHEST)
    iterate = projected / jnp.sqrt(jnp.sum(projected * projected, axis=0, keepdims=True) + norm_eps)
    for sweep_index in range(ITERS):
        inner_gram = jnp.dot(iterate.T, iterate, precision=lax.Precision.HIGHEST)
        iterate = 1.5 * iterate - 0.5 * jnp.dot(
            iterate, inner_gram, precision=lax.Precision.HIGHEST
        )
    return quantize(iterate)


def local(grad_parts, owner_map, apply_map, gram_old, old_vectors):
    fsdp_size = lax.axis_size("fsdp")
    data_size = lax.axis_size("dp")
    per_range = owner_map.shape[0] // data_size
    stripe_rows = grad_parts.shape[2]
    extent = grad_parts.shape[3]
    data_index = lax.axis_index("dp")
    summed = lax.psum_scatter(grad_parts[0], "dp", scatter_dimension=0, tiled=True).astype(
        jnp.float32
    )
    local_rows = summed.astype(jnp.bfloat16).reshape(per_range, stripe_rows * extent)
    owners = lax.dynamic_slice_in_dim(owner_map, data_index * per_range, per_range)
    rank_ids = jnp.arange(fsdp_size, dtype=jnp.int32)
    positions = jnp.arange(per_range, dtype=jnp.int32)
    owns_table = owners[None, :] == rank_ids[:, None]
    has_block = jnp.any(owns_table, axis=1)
    block_of = jnp.sum(jnp.where(owns_table, positions[None, :], 0), axis=1)
    outgoing = jnp.dot(
        owns_table.astype(jnp.bfloat16), local_rows, preferred_element_type=jnp.float32
    )
    outgoing = outgoing.astype(jnp.bfloat16).reshape(fsdp_size * stripe_rows, extent)
    gradient = lax.all_to_all(outgoing, "fsdp", split_axis=0, concat_axis=0, tiled=True)
    states = gram_old[0, 0]
    old_bases = old_vectors[0, 0]
    left_side = refresh(gradient, states[0], old_bases[0])
    right_side = refresh(gradient.T, states[1], old_bases[1])
    code_tiles = jnp.stack([left_side[0], right_side[0]])
    scales = jnp.stack([left_side[1], right_side[1]])
    side_ids = jnp.arange(2, dtype=jnp.int32)
    source_ids = jnp.where(
        has_block[:, None], 2 * block_of[:, None] + side_ids[None, :], -1
    ).reshape(2 * fsdp_size)
    got_codes, got_scales = (
        lax.all_to_all(code_tiles, "fsdp", split_axis=1, concat_axis=0, tiled=True),
        lax.all_to_all(scales, "fsdp", split_axis=1, concat_axis=0, tiled=True),
    )
    factor_count = 2 * per_range
    apply_ranks = lax.dynamic_slice_in_dim(apply_map, data_index * per_range, per_range).reshape(
        factor_count
    )
    factor_ids = jnp.arange(factor_count, dtype=jnp.int32)
    same_rank = apply_ranks[:, None] == apply_ranks[None, :]
    slot_index = jnp.sum(
        (same_rank & (factor_ids[None, :] < factor_ids[:, None])).astype(jnp.int32), axis=1
    )
    slot_rows = jnp.arange(AP_CAP * fsdp_size, dtype=jnp.int32)
    slot_number = slot_rows // fsdp_size
    slot_rank = slot_rows % fsdp_size
    matches = (apply_ranks[None, :] == slot_rank[:, None]) & (
        slot_index[None, :] == slot_number[:, None]
    )
    wanted = jnp.where(
        jnp.any(matches, axis=1), jnp.sum(jnp.where(matches, factor_ids[None, :], 0), axis=1), -2
    )
    selector = wanted[:, None] == source_ids[None, :]
    sources = got_codes.shape[0]
    sent_codes = jnp.dot(
        selector.astype(jnp.bfloat16),
        got_codes.reshape(sources, stripe_rows * extent),
        preferred_element_type=jnp.float32,
    )
    sent_codes = sent_codes.astype(jnp.bfloat16).reshape(AP_CAP, fsdp_size * stripe_rows, extent)
    sent_scales = jnp.dot(
        selector.astype(jnp.bfloat16),
        got_scales.reshape(sources, stripe_rows * (extent // QG)),
        preferred_element_type=jnp.float32,
    )
    sent_scales = sent_scales.astype(jnp.bfloat16).reshape(
        AP_CAP, fsdp_size * stripe_rows, extent // QG
    )
    final_codes, final_scales = (
        lax.all_to_all(sent_codes, "fsdp", split_axis=1, concat_axis=1, tiled=True),
        lax.all_to_all(sent_scales, "fsdp", split_axis=1, concat_axis=1, tiled=True),
    )
    return (final_codes[None, None], final_scales[None, None])


def solution(mesh):
    placed = (
        P("dp", None, "fsdp", None),
        P(),
        P(),
        P("dp", "fsdp", None, None, None),
        P("dp", "fsdp", None, None, None),
    )
    return jax.shard_map(
        local,
        mesh=mesh,
        in_specs=placed,
        out_specs=(P("dp", "fsdp", None, None, None), P("dp", "fsdp", None, None, None)),
        check_vma=False,
    )
```

profile of v0, /device:TPU:1, one launch (start us, length us, event | category | flops | bytes accessed | tf_op | source)
XLA Modules:
  0.0 225.1 jit_solution(18243430884098113831)
XLA Ops:
  8.0 49.1 %reduce-scatter.2.cloned.1.call-done = bf16[28,8,512]{2,1,0:T(8,128)(2,1)} async-done(((bf16[224,8,512]{2,1,0:T(8,128)(2,1)}), bf16[28,8,512]{2,1,0:T(8,128)(2,1)}) %reduce-scatter.2.cloned.1.call-update) | async-done | bytes 229392 | tf_op jit(solution)/shard_map/reduce_scatter | solution.py:43
  58.8 31.5 %all_to_all.52 = bf16[64,8,512]{2,1,0:T(8,128)(2,1)S(1)} all-to-all(bf16[64,8,512]{2,1,0:T(8,128)(2,1)S(1)} %bitcast.88), channel_id=1, replica_groups=mesh['dp'=8,'fsdp'=64] {'fsdp'}, dimensions={0} | all-to-all | bytes 1048576 | tf_op jit(solution)/shard_map/all_to_all | solution.py:57
  91.5 1.2 multiply_reduce_fusion
  93.1 1.2 multiply_reduce_fusion.1
  94.3 2.0 fusion.16
  96.3 2.2 fusion.4
  98.5 1.9 fusion.32
  100.4 2.0 bitcast_reduce_fusion.1
  102.4 2.2 fusion.17
  104.6 2.1 fusion.1
  106.7 1.9 fusion.33
  108.6 2.0 bitcast_reduce_fusion
  111.5 6.3 %all-to-all-start.3 = ((bf16[2,512,8]{2,0,1:T(2,128)(2,1)}), bf16[2,512,8]{2,0,1:T(2,128)(2,1)S(1)}, u32[]{:S(2)}, u32[]{:S(2)}) async-start(bf16[2,512,8]{2,0,1:T(2,128)(2,1)} %copy.45), calls=%async_computation.4 | async-start | bytes 524288 | tf_op jit(solution)/shard_map/all_to_all | solution.py:70
  118.1 2.1 copy.41
  120.2 9.5 %all-to-all-done.3 = bf16[2,512,8]{2,0,1:T(2,128)(2,1)S(1)} async-done(((bf16[2,512,8]{2,0,1:T(2,128)(2,1)}), bf16[2,512,8]{2,0,1:T(2,128)(2,1)S(1)}, u32[]{:S(2)}, u32[]{:S(2)}) %all-to-all-start.3) | async-done | bytes 16416 | tf_op jit(solution)/shard_map/all_to_all | solution.py:70
  129.8 6.0 %all-to-all-start.1 = ((bf16[2,512,512]{2,0,1:T(2,128)(2,1)}), bf16[2,512,512]{2,0,1:T(2,128)(2,1)S(1)}, u32[]{:S(2)}, u32[]{:S(2)}) async-start(bf16[2,512,512]{2,0,1:T(2,128)(2,1)} %copy.41), calls=%async_computation.2 | async-start | bytes 2097152 | tf_op jit(solution)/shard_map/all_to_all | solution.py:69
  137.7 1.0 copy.49
  138.7 25.7 %all-to-all-done.1 = bf16[2,512,512]{2,0,1:T(2,128)(2,1)S(1)} async-done(((bf16[2,512,512]{2,0,1:T(2,128)(2,1)}), bf16[2,512,512]{2,0,1:T(2,128)(2,1)S(1)}, u32[]{:S(2)}, u32[]{:S(2)}) %all-to-all-start.1) | async-done | bytes 1048608 | tf_op jit(solution)/shard_map/all_to_all | solution.py:69
  164.3 6.2 %all-to-all-start.4 = ((bf16[2,512,8]{2,0,1:T(2,128)(2,1)}), bf16[2,512,8]{2,0,1:T(2,128)(2,1)S(1)}, u32[]{:S(2)}, u32[]{:S(2)}) async-start(bf16[2,512,8]{2,0,1:T(2,128)(2,1)} %copy.49), calls=%async_computation.5 | async-start | bytes 524288 | tf_op jit(solution)/shard_map/all_to_all | solution.py:108
  172.3 2.0 copy.44
  174.4 8.2 %all-to-all-done.4 = bf16[2,512,8]{2,0,1:T(2,128)(2,1)S(1)} async-done(((bf16[2,512,8]{2,0,1:T(2,128)(2,1)}), bf16[2,512,8]{2,0,1:T(2,128)(2,1)S(1)}, u32[]{:S(2)}, u32[]{:S(2)}) %all-to-all-start.4) | async-done | bytes 16416 | tf_op jit(solution)/shard_map/all_to_all | solution.py:108
  182.6 6.0 %all-to-all-start.2 = ((bf16[2,512,512]{2,0,1:T(2,128)(2,1)}), bf16[2,512,512]{2,0,1:T(2,128)(2,1)S(1)}, u32[]{:S(2)}, u32[]{:S(2)}) async-start(bf16[2,512,512]{2,0,1:T(2,128)(2,1)} %copy.44), calls=%async_computation.3 | async-start | bytes 2097152 | tf_op jit(solution)/shard_map/all_to_all | solution.py:107
  189.3 27.8 %all-to-all-done.2 = bf16[2,512,512]{2,0,1:T(2,128)(2,1)S(1)} async-done(((bf16[2,512,512]{2,0,1:T(2,128)(2,1)}), bf16[2,512,512]{2,0,1:T(2,128)(2,1)S(1)}, u32[]{:S(2)}, u32[]{:S(2)}) %all-to-all-start.2) | async-done | bytes 1048608 | tf_op jit(solution)/shard_map/all_to_all | solution.py:107
  217.1 1.1 copy.50
  (49 shorter events, 9.7 us)
Async XLA Ops:
  7.2 128.6 %copy-start = (s32[224,2]{0,1:T(2,128)S(1)}, s32[224,2]{0,1:T(2,128)}, u32[]{:S(2)}) copy-start(s32[224,2]{0,1:T(2,128)} %param.7) | copy-start | bytes 5380
  7.2 0.8 copy-start.3
  7.2 49.9 %reduce-scatter.2.cloned.1.call-start = ((), (), s32[]{:S(2)}) async-start(), calls=%async_computation.6 | async-start | bytes 2064384 | tf_op jit(solution)/shard_map/reduce_scatter | solution.py:43
  8.0 82.2 %copy-start.2 = (bf16[1,1,2,512,512]{4,3,2,1,0:T(8,128)(2,1)S(1)}, bf16[1,1,2,512,512]{4,3,2,1,0:T(8,128)(2,1)}, u32[]{:S(2)}) copy-start(bf16[1,1,2,512,512]{4,3,2,1,0:T(8,128)(2,1)} %param.8) | copy-start | bytes 3145732
  90.2 1.2 copy-start.1
  111.5 18.3 %all-to-all-start.3 = ((bf16[2,512,8]{2,0,1:T(2,128)(2,1)}), bf16[2,512,8]{2,0,1:T(2,128)(2,1)S(1)}, u32[]{:S(2)}, u32[]{:S(2)}) async-start(bf16[2,512,8]{2,0,1:T(2,128)(2,1)} %copy.45), calls=%async_computation.4 | async-start | bytes 524288 | tf_op jit(solution)/shard_map/all_to_all | solution.py:70
  129.8 34.6 %all-to-all-start.1 = ((bf16[2,512,512]{2,0,1:T(2,128)(2,1)}), bf16[2,512,512]{2,0,1:T(2,128)(2,1)S(1)}, u32[]{:S(2)}, u32[]{:S(2)}) async-start(bf16[2,512,512]{2,0,1:T(2,128)(2,1)} %copy.41), calls=%async_computation.2 | async-start | bytes 2097152 | tf_op jit(solution)/shard_map/all_to_all | solution.py:69
  164.3 18.2 %all-to-all-start.4 = ((bf16[2,512,8]{2,0,1:T(2,128)(2,1)}), bf16[2,512,8]{2,0,1:T(2,128)(2,1)S(1)}, u32[]{:S(2)}, u32[]{:S(2)}) async-start(bf16[2,512,8]{2,0,1:T(2,128)(2,1)} %copy.49), calls=%async_computation.5 | async-start | bytes 524288 | tf_op jit(solution)/shard_map/all_to_all | solution.py:108
  182.6 34.6 %all-to-all-start.2 = ((bf16[2,512,512]{2,0,1:T(2,128)(2,1)}), bf16[2,512,512]{2,0,1:T(2,128)(2,1)S(1)}, u32[]{:S(2)}, u32[]{:S(2)}) async-start(bf16[2,512,512]{2,0,1:T(2,128)(2,1)} %copy.44), calls=%async_computation.3 | async-start | bytes 2097152 | tf_op jit(solution)/shard_map/all_to_all | solution.py:107
Sparse Core Ops, SparseCore 0:
  10.9 46.1 reduce-scatter.1
where the time goes:
time: 226 us; the launch traced here: 225 us
  waiting for transfers between devices  121 us (54%)
  blocking collectives  31.5 us (14%)
  starting transfers between devices  24.6 us (11%)
  matrix products  20.6 us (9%)
  between operations  14.3 us (6%)
  local copies, waits for them, and re-layouts  12.1 us (5%)
    reduce_scatter x1, waiting for transfers between devices, local(): lax.psum_scatter(grad_parts[0], 'dp', scatter_dimension=0, tiled=True)  49.1 us
    all_to_all x1, blocking collectives, local(): lax.all_to_all(outgoing, 'fsdp', split_axis=0, concat_axis=0, tiled=True)  31.5 us
    all_to_all x1, waiting for transfers between devices, local(): lax.all_to_all(sent_codes, 'fsdp', split_axis=1, concat_axis=1, tiled=True)  27.8 us
    all_to_all x1, waiting for transfers between devices, local(): lax.all_to_all(code_tiles, 'fsdp', split_axis=1, concat_axis=0, tiled=True)  25.7 us
    all_to_all x1, waiting for transfers between devices, local(): lax.all_to_all(scales, 'fsdp', split_axis=1, concat_axis=0, tiled=True)  9.51 us
    dot_general x4, matrix products, refresh(): jnp.dot(iterate, inner_gram, precision=lax.Precision.HIGHEST)  8.3 us
    all_to_all x1, waiting for transfers between devices, local(): lax.all_to_all(sent_scales, 'fsdp', split_axis=1, concat_axis=1, tiled=True)  8.19 us
    dot_general x4, matrix products, refresh(): inner_gram = jnp.dot(iterate.T, iterate, precision=lax.Precision.HIGHEST)  7.91 us
  transfers between devices with their start and end apart: 5, of which 5 were waited for; matrix products, arithmetic and copies ran while one was open for 4% of the time, Pallas kernels for 0%

commit v1 on v0

v1 whole, which is shorter than its diff:
```python
import functools

import jax
import jax.numpy as jnp
from jax import lax
from jax.experimental import pallas as pl
from jax.experimental.pallas import tpu as pltpu
from jax.sharding import PartitionSpec as P

QG = 64
ITERS = 2
AP_CAP = 2
MESH = pl.DeviceIdType.MESH

ema_decay = 0.95
norm_eps = 1e-06

N_CHUNK = 4
F32 = jnp.float32
BF16 = jnp.bfloat16


def dot_nn(a, b):
    return jnp.dot(a, b, preferred_element_type=F32)


def dot_nt(a, b):
    return lax.dot_general(a, b, (((1,), (1,)), ((), ())), preferred_element_type=F32)


def split(value):
    high = value.astype(BF16)
    return high, (value - high.astype(F32)).astype(BF16)


def wait_bytes(ref, sem):
    pltpu.make_async_copy(ref, ref, sem).wait()


def kernel(
    n_dp, n_fsdp, per_range,
    table, grads, grams, vectors,
    codes_out, scales_out,
    grad_v, sums_up, sums_down, summed, outgoing, stripes,
    gram_own, vec_own, gram_far, vec_far, iterate_m, held, chosen, landed, scale_m,
    load_sem, far_send, far_recv, up_send, up_recv, down_send, down_recv,
    first_send, first_recv, second_send, second_recv, third_send, third_recv,
):
    dp = lax.axis_index("dp")
    me = lax.axis_index("fsdp")
    half_count = n_fsdp // 2
    side = me // half_count
    extent = gram_own.shape[0]
    width = extent // N_CHUNK
    piece_rows, piece_cols = held.shape[1], held.shape[2]
    group = 8

    loads = [
        pltpu.make_async_copy(grads, grad_v, load_sem.at[0]),
        pltpu.make_async_copy(grams.at[side], gram_own, load_sem.at[1]),
        pltpu.make_async_copy(vectors.at[side], vec_own, load_sem.at[2]),
    ]
    for load in loads:
        load.start()

    barrier = pltpu.get_barrier_semaphore()

    def greet(k, carry):
        pl.semaphore_signal(barrier, inc=1, device_id={"fsdp": me ^ k}, device_id_type=MESH)
        return carry

    up = lax.rem(dp + 1, n_dp)
    down = lax.rem(dp + n_dp - 1, n_dp)
    pl.semaphore_signal(barrier, inc=1, device_id={"dp": up}, device_id_type=MESH)
    pl.semaphore_signal(barrier, inc=1, device_id={"dp": down}, device_id_type=MESH)
    lax.fori_loop(1, n_fsdp, greet, 0)
    pl.semaphore_wait(barrier, n_fsdp + 1)

    mate = lax.rem(me + half_count, n_fsdp)
    n_band = 4
    band = extent // n_band
    swaps = [
        pltpu.make_async_remote_copy(
            src_ref=vectors.at[1 - side], dst_ref=vec_far,
            send_sem=far_send.at[n_band], recv_sem=far_recv.at[n_band],
            device_id={"fsdp": mate}, device_id_type=MESH,
        )
    ]
    for i in range(n_band):
        rows, cols = pl.ds(i * band, band), pl.ds(i * band, extent - i * band)
        swaps.append(
            pltpu.make_async_remote_copy(
                src_ref=grams.at[1 - side, rows, cols], dst_ref=gram_far.at[rows, cols],
                send_sem=far_send.at[i], recv_sem=far_recv.at[i],
                device_id={"fsdp": mate}, device_id_type=MESH,
            )
        )

    half = per_range // 2
    far_off = n_dp // 2
    ways = (
        (1, up, sums_up, up_send, up_recv, pl.ds(0, half)),
        (-1, down, sums_down, down_send, down_recv, pl.ds(half, per_range - half)),
    )

    def columns(c):
        return pl.ds(c * width, width)

    def ring_copy(way, c, step):
        sign, target, sums, send, recv, part = way
        dest = lax.rem(dp + sign * (far_off - step) + n_dp, n_dp)
        if step == 0:
            src = grad_v.at[dest, part, :, columns(c)]
            dst = sums.at[0, part, :, columns(c)]
        else:
            src = sums.at[step - 1, :, :, columns(c)]
            dst = sums.at[step, :, :, columns(c)]
        return pltpu.make_async_remote_copy(
            src_ref=src, dst_ref=dst, send_sem=send.at[c, step], recv_sem=recv.at[c, step],
            device_id={"dp": target}, device_id_type=MESH,
        )

    def ring_step(c, step):
        for way in ways:
            sign, target, sums, send, recv, part = way
            if step > 0:
                ring_copy(way, c, step - 1).wait_recv()
                dest = lax.rem(dp + sign * (far_off - step) + n_dp, n_dp)
                if step == 1:
                    other = pl.ds(half, per_range - half) if sign == 1 else pl.ds(0, half)
                    sums[0, part, :, columns(c)] = (
                        sums[0, part, :, columns(c)].astype(F32)
                        + grad_v[dest, part, :, columns(c)].astype(F32)
                    ).astype(BF16)
                    sums[0, other, :, columns(c)] = grad_v[dest, other, :, columns(c)]
                else:
                    sums[step - 1, :, :, columns(c)] = (
                        sums[step - 1, :, :, columns(c)].astype(F32)
                        + grad_v[dest, :, :, columns(c)].astype(F32)
                    ).astype(BF16)
            ring_copy(way, c, step).start()

    def finish(c):
        for way in ways:
            ring_copy(way, c, far_off - 1).wait_recv()
        total = (
            grad_v[dp, :, :, columns(c)].astype(F32)
            + sums_up[far_off - 1, :, :, columns(c)].astype(F32)
            + sums_down[far_off - 1, :, :, columns(c)].astype(F32)
        )
        summed[c] = total.astype(BF16)

        def pick(p, carry):
            outgoing[c, p] = summed[c, table[p]]
            return carry

        lax.fori_loop(0, half_count, pick, 0)

        def post(k, carry):
            target = me ^ k
            pltpu.make_async_remote_copy(
                src_ref=outgoing.at[c, lax.rem(target, half_count)],
                dst_ref=stripes.at[me, :, columns(c)],
                send_sem=first_send, recv_sem=first_recv.at[c],
                device_id={"fsdp": target}, device_id_type=MESH,
            ).start()
            return carry

        lax.fori_loop(1, n_fsdp, post, 0)
        stripes[me, :, columns(c)] = outgoing[c, lax.rem(me, half_count)]

    loads[0].wait()
    for c in range(N_CHUNK):
        ring_step(c, 0)
    for swap in swaps:
        swap.start()
    order = sorted(
        (2 * c + step, -step, c, step) for c in range(N_CHUNK) for step in range(1, far_off + 1)
    )
    for _, _, c, step in order:
        if step < far_off:
            ring_step(c, step)
        else:
            finish(c)

    loads[1].wait()
    loads[2].wait()
    for swap in swaps:
        swap.wait_recv()
    owns = table[half_count + AP_CAP * n_fsdp] > 0
    basis = jnp.where(owns, vec_own[...], vec_far[...]).T
    for i in range(n_band):
        for j in range(i, n_band):
            rows, cols = pl.ds(i * band, band), pl.ds(j * band, band)
            tile = jnp.where(owns, gram_own[rows, cols], gram_far[rows, cols])
            gram_own[rows, cols] = tile
            if j > i:
                gram_own[cols, rows] = tile.T
    for c in range(N_CHUNK):
        wait_bytes(stripes.at[pl.ds(0, n_fsdp - 1), :, columns(c)], first_recv.at[c])
    block = stripes[...].astype(F32).reshape(extent, extent)

    @pl.when(side == 0)
    def _():
        iterate_m[...] = block.astype(BF16)

    @pl.when(side == 1)
    def _():
        iterate_m[...] = block.T.astype(BF16)

    matrix = iterate_m[...]
    state = ema_decay * gram_own[...].astype(F32) + (1.0 - ema_decay) * dot_nt(matrix, matrix)
    state_high, state_low = split(state)
    turned = dot_nn(basis, state_high) + dot_nn(basis, state_low)
    turned = turned / jnp.sqrt(jnp.sum(turned * turned, axis=1, keepdims=True) + norm_eps)
    for _ in range(ITERS):
        high, low = split(turned)
        inner = dot_nt(high, high) + dot_nt(high, low) + dot_nt(low, high)
        inner_high, inner_low = split(inner)
        turned = 1.5 * turned - 0.5 * (
            dot_nn(inner_high, high) + dot_nn(inner_high, low) + dot_nn(inner_low, high)
        )
    iterate_m[...] = turned.T.astype(BF16)

    def piece(i):
        return (
            pl.ds(pl.multiple_of((i // 2) * piece_rows, piece_rows), piece_rows),
            pl.ds(pl.multiple_of(lax.rem(i, 2) * piece_cols, piece_cols), piece_cols),
        )

    def spread(k, carry):
        target = me ^ k
        pltpu.make_async_remote_copy(
            src_ref=iterate_m.at[piece(target)], dst_ref=held.at[me],
            send_sem=second_send, recv_sem=second_recv,
            device_id={"fsdp": target}, device_id_type=MESH,
        ).start()
        return carry

    lax.fori_loop(1, n_fsdp, spread, 0)
    held[me] = iterate_m[piece(me)]
    held[n_fsdp] = jnp.zeros((piece_rows, piece_cols), BF16)
    wait_bytes(held.at[pl.ds(0, n_fsdp - 1)], second_recv)

    def select(target, place):
        for t in range(AP_CAP):
            place[target, t] = held[table[half_count + t * n_fsdp + target]]

    def deliver(k, carry):
        target = me ^ k
        select(target, chosen)
        pltpu.make_async_remote_copy(
            src_ref=chosen.at[target], dst_ref=landed.at[me],
            send_sem=third_send, recv_sem=third_recv.at[k // group],
            device_id={"fsdp": target}, device_id_type=MESH,
        ).start()
        return carry

    lax.fori_loop(1, n_fsdp, deliver, 0)
    select(me, landed)

    lane = lax.broadcasted_iota(jnp.int32, (piece_rows, 128), 1)

    def quantize(m, carry):
        pair = (me // 2) ^ m
        rows = pl.ds(pl.multiple_of(pair * piece_rows, piece_rows), piece_rows)
        for t in range(AP_CAP):
            filled = table[half_count + t * n_fsdp + me] < n_fsdp
            scales = jnp.zeros((piece_rows, 128), F32)
            for h in range(2):
                for q in range(piece_cols // 128):
                    value = landed[2 * pair + h, t, :, pl.ds(q * 128, 128)].astype(F32)
                    size = jnp.abs(value)
                    first = jnp.max(jnp.where(lane < QG, size, 0.0), axis=1, keepdims=True)
                    last = jnp.max(jnp.where(lane < QG, 0.0, size), axis=1, keepdims=True)
                    first = (first + norm_eps).astype(BF16).astype(F32)
                    last = (last + norm_eps).astype(BF16).astype(F32)
                    code = value / jnp.where(lane < QG, first, last)
                    at = h * piece_cols + q * 128
                    codes_out[t, rows, pl.ds(at, 128)] = code.astype(BF16)
                    place = at // QG
                    scales = jnp.where(lane == place, first, scales)
                    scales = jnp.where(lane == place + 1, last, scales)
            scale_m[t, rows, :] = jnp.where(filled, scales, 0.0)
        return carry

    for g in range(n_fsdp // group):
        count = group - 1 if g == 0 else group
        wait_bytes(landed.at[pl.ds(0, count)], third_recv.at[g])
        lax.fori_loop(g * group // 2, (g + 1) * group // 2, quantize, 0)
    n_group = extent // QG
    for t in range(AP_CAP):
        scales_out[t] = scale_m[t].T[:n_group].astype(BF16)

    for swap in swaps:
        swap.wait_send()
    for c in range(N_CHUNK):
        for step in range(far_off):
            for way in ways:
                ring_copy(way, c, step).wait_send()
    for c in range(N_CHUNK):
        wait_bytes(stripes.at[pl.ds(0, n_fsdp - 1), :, columns(c)], first_send)
    wait_bytes(held.at[pl.ds(0, n_fsdp - 1)], second_send)
    wait_bytes(landed.at[pl.ds(0, n_fsdp - 1)], third_send)


def make_table(owner_map, apply_map, n_dp, n_fsdp):
    per_range = owner_map.shape[0] // n_dp
    half_count = n_fsdp // 2
    dp = lax.axis_index("dp")
    me = lax.axis_index("fsdp")
    owners = lax.dynamic_slice_in_dim(owner_map, dp * per_range, per_range)
    ranks = lax.dynamic_slice_in_dim(apply_map, dp * per_range, per_range).reshape(2 * per_range)
    pairs = owners % half_count
    at_pair = pairs[None, :] == jnp.arange(half_count, dtype=jnp.int32)[:, None]
    block_of = jnp.sum(
        jnp.where(at_pair, jnp.arange(per_range, dtype=jnp.int32)[None, :], 0), axis=1
    )
    sources = (
        pairs[:, None] + half_count * jnp.arange(2, dtype=jnp.int32)[None, :]
    ).reshape(2 * per_range)
    ids = jnp.arange(2 * per_range, dtype=jnp.int32)
    slots = jnp.sum(
        ((ranks[:, None] == ranks[None, :]) & (ids[None, :] < ids[:, None])).astype(jnp.int32),
        axis=1,
    )
    places = slots * n_fsdp + ranks
    wanted = places[None, :] == jnp.arange(AP_CAP * n_fsdp, dtype=jnp.int32)[:, None]
    select = n_fsdp - jnp.sum(jnp.where(wanted, n_fsdp - sources[None, :], 0), axis=1)
    owns = jnp.any(owners == me).astype(jnp.int32)
    return jnp.concatenate([block_of, select, owns[None]]).astype(jnp.int32)


def local(grad_parts, owner_map, apply_map, gram_old, old_vectors):
    n_dp = lax.axis_size("dp")
    n_fsdp = lax.axis_size("fsdp")
    per_range = owner_map.shape[0] // n_dp
    stripe, extent = grad_parts.shape[2], grad_parts.shape[3]
    table = make_table(owner_map, apply_map, n_dp, n_fsdp)
    grads = grad_parts.reshape(n_dp, per_range, stripe, extent)
    far_off = n_dp // 2
    width = extent // N_CHUNK
    piece = (extent * 2 // n_fsdp, extent // 2)
    vmem, dma = pltpu.VMEM, pltpu.SemaphoreType.DMA
    codes, scales = pl.pallas_call(
        functools.partial(kernel, n_dp, n_fsdp, per_range),
        out_shape=(
            jax.ShapeDtypeStruct((AP_CAP, extent, extent), BF16),
            jax.ShapeDtypeStruct((AP_CAP, extent // QG, extent), BF16),
        ),
        in_specs=[pl.BlockSpec(memory_space=pltpu.SMEM)] + [pl.BlockSpec(memory_space=pl.ANY)] * 3,
        out_specs=(pl.BlockSpec(memory_space=pltpu.VMEM), pl.BlockSpec(memory_space=pltpu.VMEM)),
        scratch_shapes=[
            vmem((n_dp, per_range, stripe, extent), BF16),
            vmem((far_off, per_range, stripe, extent), BF16),
            vmem((far_off, per_range, stripe, extent), BF16),
            vmem((N_CHUNK, per_range, stripe, width), BF16),
            vmem((N_CHUNK, n_fsdp // 2, stripe, width), BF16),
            vmem((n_fsdp, stripe, extent), BF16),
            vmem((extent, extent), BF16),
            vmem((extent, extent), BF16),
            vmem((extent, extent), BF16),
            vmem((extent, extent), BF16),
            vmem((extent, extent), BF16),
            vmem((n_fsdp + 1,) + piece, BF16),
            vmem((n_fsdp, AP_CAP) + piece, BF16),
            vmem((n_fsdp, AP_CAP) + piece, BF16),
            vmem((AP_CAP, extent, 128), F32),
            dma((3,)),
            dma((5,)), dma((5,)),
            dma((N_CHUNK, far_off)), dma((N_CHUNK, far_off)),
            dma((N_CHUNK, far_off)), dma((N_CHUNK, far_off)),
            dma, dma((N_CHUNK,)),
            dma, dma,
            dma, dma((n_fsdp // 8,)),
        ],
        compiler_params=pltpu.CompilerParams(
            collective_id=0, has_side_effects=True, vmem_limit_bytes=48 * 2**20
        ),
        name="refresh",
    )(table, grads, gram_old[0, 0], old_vectors[0, 0])
    return codes[None, None], jnp.swapaxes(scales, 1, 2)[None, None]


def solution(mesh):
    placed = (
        P("dp", None, "fsdp", None),
        P(),
        P(),
        P("dp", "fsdp", None, None, None),
        P("dp", "fsdp", None, None, None),
    )
    return jax.shard_map(
        local,
        mesh=mesh,
        in_specs=placed,
        out_specs=(P("dp", "fsdp", None, None, None), P("dp", "fsdp", None, None, None)),
        check_vma=False,
    )
```

time: 226 us -> 122 us (0.54)
  waiting for transfers between devices: 121 us -> 0 us
  Pallas kernels: 0 us -> 112 us
  blocking collectives: 31.5 us -> 0 us
  starting transfers between devices: 24.6 us -> 0 us
  matrix products: 20.6 us -> 0 us
  between operations: 14.3 us -> 1.33 us
  local copies, waits for them, and re-layouts: 12.1 us -> 5.92 us
    pallas_call x0 -> x1, Pallas kernels: none -> 112 us  [local(): pl.pallas_call(functools.partial(kernel, n_dp, n_fsdp, per_range), out_sh...]
    all_to_all x4 -> x0, waiting for transfers between devices: 71.2 us -> none  [the longest x1 27.8 us: local(): lax.all_to_all(sent_codes, 'fsdp', split_axis=1, concat_axis=1, tiled=True)]
    reduce_scatter x1 -> x0, waiting for transfers between devices: 49.1 us -> none  [local(): lax.psum_scatter(grad_parts[0], 'dp', scatter_dimension=0, tiled=True)]
    all_to_all x1 -> x0, blocking collectives: 31.5 us -> none  [local(): lax.all_to_all(outgoing, 'fsdp', split_axis=0, concat_axis=0, tiled=True)]
    all_to_all x4 -> x0, starting transfers between devices: 24.5 us -> none  [the longest x1 6.28 us: local(): lax.all_to_all(scales, 'fsdp', split_axis=1, concat_axis=0, tiled=True)]
    dot_general x15 -> x0, matrix products: 20.6 us -> none  [the longest x4 8.3 us: refresh(): jnp.dot(iterate, inner_gram, precision=lax.Precision.HIGHEST)]
    reshape x5 -> x0, local copies, waits for them, and re-layouts: 3.94 us -> none  [the longest x2 2.58 us: local(): sent_codes.astype(jnp.bfloat16)]
    another operation x2 -> x0, local copies, waits for them, and re-layouts: 2.96 us -> none  [the longest x1 2.1 us: local(): code_tiles = jnp.stack([left_side[0], right_side[0]])]
  transfers between devices with their start and end apart: 5 -> 0, of which waited for: 5 -> 0; matrix products, arithmetic and copies ran while one was open for 4% -> 0% of each run, Pallas kernels for 0% -> 0%
where the time goes in v1:
time: 122 us
  Pallas kernels  112 us (92%)
  local copies, waits for them, and re-layouts  5.92 us (5%)
  other arithmetic  2.72 us (2%)
  between operations  1.33 us (1%)
    pallas_call x1, Pallas kernels, local(): pl.pallas_call(functools.partial(kernel, n_dp, n_fsdp, per_range), out_sh...  112 us
    unnamed x10, local copies, waits for them, and re-layouts  5.54 us

profile of v1, /device:TPU:1, one launch (start us, length us, event | category | flops | bytes accessed | tf_op | source)
XLA Modules:
  0.0 122.1 jit_solution(15855075773153671350)
XLA Ops:
  0.6 0.0 copy-start
  0.7 1.4 %compare_reduce_fusion = pred[]{:T(512)} fusion(s32[]{:T(128)S(6)} %axis_index.25, s32[224]{0:T(256)} %param.6, s32[]{:T(128)S(6)} %select_n.19), kind=kLoop, calls=%fused_computation.10 | loop fusion | flops 55 | bytes 121 | tf_op jit(solution)/shard_map/reduce_or | solution.py:330
  2.7 0.8 and_select_fusion
  3.5 0.0 copy-done
  3.5 0.1 constant_dynamic-slice_fusion
  3.5 0.1 select_reduce_fusion.1
  3.7 0.1 add_subtract_fusion
  3.7 0.1 sub.20
  3.8 0.1 copy.9
  3.9 0.1 eq.52
  4.0 0.2 convert_reduce_fusion
  4.2 0.1 select_reduce_fusion
  4.3 0.1 pad_add_fusion.table
  4.4 0.0 copy-start.1
  4.4 1.5 %copy-done.1 = bf16[1,224,8,512]{3,2,1,0:T(8,128)(2,1)S(1)} copy-done((bf16[1,224,8,512]{3,2,1,0:T(8,128)(2,1)S(1)}, bf16[1,224,8,512]{3,2,1,0:T(8,128)(2,1)}, u32[]{:S(2)}) %copy-start.1) | copy-done | bytes 1835032
  5.9 0.0 copy-start.2
  5.9 1.2 %copy-done.2 = bf16[1,1,2,512,512]{4,3,2,1,0:T(8,128)(2,1)S(1)} copy-done((bf16[1,1,2,512,512]{4,3,2,1,0:T(8,128)(2,1)S(1)}, bf16[1,1,2,512,512]{4,3,2,1,0:T(8,128)(2,1)}, u32[]{:S(2)}) %copy-start.2) | copy-done | bytes 1048600
  7.2 0.0 copy-start.3
  7.2 1.2 %copy-done.3 = bf16[1,1,2,512,512]{4,3,2,1,0:T(8,128)(2,1)S(1)} copy-done((bf16[1,1,2,512,512]{4,3,2,1,0:T(8,128)(2,1)S(1)}, bf16[1,1,2,512,512]{4,3,2,1,0:T(8,128)(2,1)}, u32[]{:S(2)}) %copy-start.3) | copy-done | bytes 1048600
  8.4 112.1 %refresh.1 = (bf16[2,512,512]{2,1,0:T(8,128)(2,1)S(1)}, bf16[2,8,512]{2,1,0:T(8,128)(2,1)S(1)}) custom-call(s32[161]{0:T(256)S(1)} %pad_add_fusion.table, bf16[8,28,8,512]{3,2,1,0:T(8,128)(2,1)S(1)} %bitcast.8, bf16[2,512,512]{2,1,0:T(8,128)(2,1)S(1)} %bitcast.9, bf16[2,512,512]{2,1,0:T(8,128)(2,1)S(1)} %bitcast.10), custom_call_target="tpu_custom_call" | custom-call | tf_op jit(solution)/shard_map/refresh/pallas_call | solution.py:345
  120.5 1.0 copy.12
  121.4 0.6 copy.13
  (3 shorter events, 0.0 us)
Async XLA Ops:
  0.6 2.8 %copy-start = (s32[224,2]{0,1:T(2,128)S(1)}, s32[224,2]{0,1:T(2,128)}, u32[]{:S(2)}) copy-start(s32[224,2]{0,1:T(2,128)} %param.7) | copy-start | bytes 5380
  4.4 1.5 %copy-start.1 = (bf16[1,224,8,512]{3,2,1,0:T(8,128)(2,1)S(1)}, bf16[1,224,8,512]{3,2,1,0:T(8,128)(2,1)}, u32[]{:S(2)}) copy-start(bf16[1,224,8,512]{3,2,1,0:T(8,128)(2,1)} %param.5) | copy-start | bytes 5505028
  5.9 1.2 %copy-start.2 = (bf16[1,1,2,512,512]{4,3,2,1,0:T(8,128)(2,1)S(1)}, bf16[1,1,2,512,512]{4,3,2,1,0:T(8,128)(2,1)}, u32[]{:S(2)}) copy-start(bf16[1,1,2,512,512]{4,3,2,1,0:T(8,128)(2,1)} %param.8) | copy-start | bytes 3145732
  7.2 1.2 %copy-start.3 = (bf16[1,1,2,512,512]{4,3,2,1,0:T(8,128)(2,1)S(1)}, bf16[1,1,2,512,512]{4,3,2,1,0:T(8,128)(2,1)}, u32[]{:S(2)}) copy-start(bf16[1,1,2,512,512]{4,3,2,1,0:T(8,128)(2,1)} %param.9) | copy-start | bytes 3145732

commit v2 on v1

--- a/solution.py
+++ b/solution.py
@@ -39,10 +39,11 @@
 
 def kernel(
     n_dp, n_fsdp, per_range,
-    table, grads, grams, vectors,
+    owner_map, apply_map, grads, grams, vectors,
     codes_out, scales_out,
+    owner_v, apply_v, table_v, table,
     grad_v, sums_up, sums_down, summed, outgoing, stripes,
-    gram_own, vec_own, gram_far, vec_far, iterate_m, held, chosen, landed, scale_m,
+    gram_own, vec_own, gram_far, vec_far, iterate_m, held_upper, held_lower, chosen, landed, scale_m,
     load_sem, far_send, far_recv, up_send, up_recv, down_send, down_recv,
     first_send, first_recv, second_send, second_recv, third_send, third_recv,
 ):
@@ -52,13 +53,17 @@
     side = me // half_count
     extent = gram_own.shape[0]
     width = extent // N_CHUNK
-    piece_rows, piece_cols = held.shape[1], held.shape[2]
+    held = (held_upper, held_lower)
+    piece_rows, piece_cols = held_upper.shape[1:]
+    across = extent // piece_cols
     group = 8
 
     loads = [
         pltpu.make_async_copy(grads, grad_v, load_sem.at[0]),
         pltpu.make_async_copy(grams.at[side], gram_own, load_sem.at[1]),
         pltpu.make_async_copy(vectors.at[side], vec_own, load_sem.at[2]),
+        pltpu.make_async_copy(owner_map, owner_v, load_sem.at[3]),
+        pltpu.make_async_copy(apply_map, apply_v, load_sem.at[4]),
     ]
     for load in loads:
         load.start()
@@ -74,6 +79,11 @@
     pl.semaphore_signal(barrier, inc=1, device_id={"dp": up}, device_id_type=MESH)
     pl.semaphore_signal(barrier, inc=1, device_id={"dp": down}, device_id_type=MESH)
     lax.fori_loop(1, n_fsdp, greet, 0)
+    loads[3].wait()
+    loads[4].wait()
+    fill_table(dp, me, half_count, per_range, owner_v, apply_v, table_v)
+    to_scalars = pltpu.make_async_copy(table_v, table, load_sem.at[5])
+    to_scalars.start()
     pl.semaphore_wait(barrier, n_fsdp + 1)
 
     mate = lax.rem(me + half_count, n_fsdp)
@@ -151,7 +161,7 @@
         summed[c] = total.astype(BF16)
 
         def pick(p, carry):
-            outgoing[c, p] = summed[c, table[p]]
+            outgoing[c, p] = summed[c, table[p, 2]]
             return carry
 
         lax.fori_loop(0, half_count, pick, 0)
@@ -172,10 +182,11 @@
     loads[0].wait()
     for c in range(N_CHUNK):
         ring_step(c, 0)
+    to_scalars.wait()
     for swap in swaps:
         swap.start()
     order = sorted(
-        (2 * c + step, -step, c, step) for c in range(N_CHUNK) for step in range(1, far_off + 1)
+        (0.5 * c + step, -step, c, step) for c in range(N_CHUNK) for step in range(1, far_off + 1)
     )
     for _, _, c, step in order:
         if step < far_off:
@@ -187,7 +198,7 @@
     loads[2].wait()
     for swap in swaps:
         swap.wait_recv()
-    owns = table[half_count + AP_CAP * n_fsdp] > 0
+    owns = table[0, 3] > 0
     basis = jnp.where(owns, vec_own[...], vec_far[...]).T
     for i in range(n_band):
         for j in range(i, n_band):
@@ -213,81 +224,99 @@
     state_high, state_low = split(state)
     turned = dot_nn(basis, state_high) + dot_nn(basis, state_low)
     turned = turned / jnp.sqrt(jnp.sum(turned * turned, axis=1, keepdims=True) + norm_eps)
-    for _ in range(ITERS):
+    for _ in range(ITERS - 1):
         high, low = split(turned)
-        inner = dot_nt(high, high) + dot_nt(high, low) + dot_nt(low, high)
-        inner_high, inner_low = split(inner)
+        inner_high, inner_low = split(dot_nt(high, high) + dot_nt(high, low) + dot_nt(low, high))
         turned = 1.5 * turned - 0.5 * (
             dot_nn(inner_high, high) + dot_nn(inner_high, low) + dot_nn(inner_low, high)
         )
-    iterate_m[...] = turned.T.astype(BF16)
-
-    def piece(i):
+    high, low = split(turned)
+    inner_high, inner_low = split(dot_nt(high, high) + dot_nt(high, low) + dot_nt(low, high))
+
+    half_rows = extent // 2
+
+    def piece(h, i):
+        row = h * half_rows + (i // across) * piece_rows
+        col = lax.rem(i, across) * piece_cols
         return (
-            pl.ds(pl.multiple_of((i // 2) * piece_rows, piece_rows), piece_rows),
-            pl.ds(pl.multiple_of(lax.rem(i, 2) * piece_cols, piece_cols), piece_cols),
-        )
-
-    def spread(k, carry):
-        target = me ^ k
-        pltpu.make_async_remote_copy(
-            src_ref=iterate_m.at[piece(target)], dst_ref=held.at[me],
-            send_sem=second_send, recv_sem=second_recv,
-            device_id={"fsdp": target}, device_id_type=MESH,
-        ).start()
-        return carry
-
-    lax.fori_loop(1, n_fsdp, spread, 0)
-    held[me] = iterate_m[piece(me)]
-    held[n_fsdp] = jnp.zeros((piece_rows, piece_cols), BF16)
-    wait_bytes(held.at[pl.ds(0, n_fsdp - 1)], second_recv)
-
-    def select(target, place):
+            pl.ds(pl.multiple_of(row, piece_rows), piece_rows),
+            pl.ds(pl.multiple_of(col, piece_cols), piece_cols),
+        )
+
+    for h in range(2):
+        part = slice(h * half_rows, (h + 1) * half_rows)
+        last = 1.5 * turned[:, part] - 0.5 * (
+            dot_nn(inner_high, high[:, part])
+            + dot_nn(inner_high, low[:, part])
+            + dot_nn(inner_low, high[:, part])
+        )
+        iterate_m[pl.ds(h * half_rows, half_rows), :] = last.T.astype(BF16)
+
+        def spread(k, carry):
+            target = me ^ k
+            pltpu.make_async_remote_copy(
+                src_ref=iterate_m.at[piece(h, target)], dst_ref=held[h].at[me],
+                send_sem=second_send, recv_sem=second_recv.at[h],
+                device_id={"fsdp": target}, device_id_type=MESH,
+            ).start()
+            return carry
+
+        lax.fori_loop(1, n_fsdp, spread, 0)
+        held[h][me] = iterate_m[piece(h, me)]
+        held[h][n_fsdp] = jnp.zeros((piece_rows, piece_cols), BF16)
+
+    def select(h, target, place):
         for t in range(AP_CAP):
-            place[target, t] = held[table[half_count + t * n_fsdp + target]]
-
-    def deliver(k, carry):
-        target = me ^ k
-        select(target, chosen)
-        pltpu.make_async_remote_copy(
-            src_ref=chosen.at[target], dst_ref=landed.at[me],
-            send_sem=third_send, recv_sem=third_recv.at[k // group],
-            device_id={"fsdp": target}, device_id_type=MESH,
-        ).start()
-        return carry
-
-    lax.fori_loop(1, n_fsdp, deliver, 0)
-    select(me, landed)
-
-    lane = lax.broadcasted_iota(jnp.int32, (piece_rows, 128), 1)
-
-    def quantize(m, carry):
-        pair = (me // 2) ^ m
-        rows = pl.ds(pl.multiple_of(pair * piece_rows, piece_rows), piece_rows)
+            place[h, target, t] = held[h][table[target, t]]
+
+    for h in range(2):
+        wait_bytes(held[h].at[pl.ds(0, n_fsdp - 1)], second_recv.at[h])
+
+        def deliver(k, carry):
+            target = me ^ k
+            select(h, target, chosen)
+            pltpu.make_async_remote_copy(
+                src_ref=chosen.at[h, target], dst_ref=landed.at[h, me],
+                send_sem=third_send, recv_sem=third_recv.at[h, k // group],
+                device_id={"fsdp": target}, device_id_type=MESH,
+            ).start()
+            return carry
+
+        lax.fori_loop(1, n_fsdp, deliver, 0)
         for t in range(AP_CAP):
-            filled = table[half_count + t * n_fsdp + me] < n_fsdp
+            landed[h, me, t] = held[h][table[me, t]]
+
+    lane = lax.broadcasted_iota(jnp.int32, (piece_rows, piece_cols), 1)
+
+    def quantize(h, m):
+        band_at = (me // across) ^ m
+        rows = pl.ds(pl.multiple_of(h * half_rows + band_at * piece_rows, piece_rows), piece_rows)
+        for t in range(AP_CAP):
+            filled = table[me, t] < n_fsdp
             scales = jnp.zeros((piece_rows, 128), F32)
-            for h in range(2):
-                for q in range(piece_cols // 128):
-                    value = landed[2 * pair + h, t, :, pl.ds(q * 128, 128)].astype(F32)
-                    size = jnp.abs(value)
-                    first = jnp.max(jnp.where(lane < QG, size, 0.0), axis=1, keepdims=True)
-                    last = jnp.max(jnp.where(lane < QG, 0.0, size), axis=1, keepdims=True)
-                    first = (first + norm_eps).astype(BF16).astype(F32)
-                    last = (last + norm_eps).astype(BF16).astype(F32)
-                    code = value / jnp.where(lane < QG, first, last)
-                    at = h * piece_cols + q * 128
-                    codes_out[t, rows, pl.ds(at, 128)] = code.astype(BF16)
-                    place = at // QG
-                    scales = jnp.where(lane == place, first, scales)
-                    scales = jnp.where(lane == place + 1, last, scales)
+            for q in range(across):
+                value = landed[h, across * band_at + q, t].astype(F32)
+                size = jnp.abs(value)
+                first = jnp.max(jnp.where(lane < QG, size, 0.0), axis=1, keepdims=True)
+                last = jnp.max(jnp.where(lane < QG, 0.0, size), axis=1, keepdims=True)
+                first = (first + norm_eps).astype(BF16).astype(F32)
+                last = (last + norm_eps).astype(BF16).astype(F32)
+                code = value / jnp.where(lane < QG, first, last)
+                codes_out[t, rows, pl.ds(q * piece_cols, piece_cols)] = code.astype(BF16)
+                scales = jnp.where(lane == 2 * q, first, scales)
+                scales = jnp.where(lane == 2 * q + 1, last, scales)
             scale_m[t, rows, :] = jnp.where(filled, scales, 0.0)
-        return carry
-
-    for g in range(n_fsdp // group):
-        count = group - 1 if g == 0 else group
-        wait_bytes(landed.at[pl.ds(0, count)], third_recv.at[g])
-        lax.fori_loop(g * group // 2, (g + 1) * group // 2, quantize, 0)
+
+    for h in range(2):
+        for g in range(n_fsdp // group):
+            count = group - 1 if g == 0 else group
+            wait_bytes(landed.at[h, pl.ds(0, count)], third_recv.at[h, g])
+
+            def several(m, carry):
+                quantize(h, m)
+                return carry
+
+            lax.fori_loop(g * group // across, (g + 1) * group // across, several, 0)
     n_group = extent // QG
     for t in range(AP_CAP):
         scales_out[t] = scale_m[t].T[:n_group].astype(BF16)
@@ -300,35 +329,35 @@
                 ring_copy(way, c, step).wait_send()
     for c in range(N_CHUNK):
         wait_bytes(stripes.at[pl.ds(0, n_fsdp - 1), :, columns(c)], first_send)
-    wait_bytes(held.at[pl.ds(0, n_fsdp - 1)], second_send)
-    wait_bytes(landed.at[pl.ds(0, n_fsdp - 1)], third_send)
-
-
-def make_table(owner_map, apply_map, n_dp, n_fsdp):
-    per_range = owner_map.shape[0] // n_dp
-    half_count = n_fsdp // 2
-    dp = lax.axis_index("dp")
-    me = lax.axis_index("fsdp")
-    owners = lax.dynamic_slice_in_dim(owner_map, dp * per_range, per_range)
-    ranks = lax.dynamic_slice_in_dim(apply_map, dp * per_range, per_range).reshape(2 * per_range)
-    pairs = owners % half_count
-    at_pair = pairs[None, :] == jnp.arange(half_count, dtype=jnp.int32)[:, None]
-    block_of = jnp.sum(
-        jnp.where(at_pair, jnp.arange(per_range, dtype=jnp.int32)[None, :], 0), axis=1
-    )
-    sources = (
-        pairs[:, None] + half_count * jnp.arange(2, dtype=jnp.int32)[None, :]
-    ).reshape(2 * per_range)
-    ids = jnp.arange(2 * per_range, dtype=jnp.int32)
-    slots = jnp.sum(
-        ((ranks[:, None] == ranks[None, :]) & (ids[None, :] < ids[:, None])).astype(jnp.int32),
-        axis=1,
-    )
-    places = slots * n_fsdp + ranks
-    wanted = places[None, :] == jnp.arange(AP_CAP * n_fsdp, dtype=jnp.int32)[:, None]
-    select = n_fsdp - jnp.sum(jnp.where(wanted, n_fsdp - sources[None, :], 0), axis=1)
-    owns = jnp.any(owners == me).astype(jnp.int32)
-    return jnp.concatenate([block_of, select, owns[None]]).astype(jnp.int32)
+    for h in range(2):
+        wait_bytes(held[h].at[pl.ds(0, n_fsdp - 1)], second_send)
+        wait_bytes(landed.at[h, pl.ds(0, n_fsdp - 1)], third_send)
+
+
+def fill_table(dp, me, half_count, per_range, owner_v, apply_v, table_v):
+    n_fsdp = 2 * half_count
+    shape = (n_fsdp, owner_v.shape[1])
+    ids = lax.broadcasted_iota(jnp.int32, shape, 1) - dp * per_range
+    ranks = lax.broadcasted_iota(jnp.int32, shape, 0)
+    ours = (ids >= 0) & (ids < per_range)
+    owners = jnp.broadcast_to(owner_v[...], shape)
+    pairs = owners & (half_count - 1)
+    none = 2 * per_range * n_fsdp
+    first = jnp.full((n_fsdp, 1), none, jnp.int32)
+    last = jnp.full((n_fsdp, 1), -1, jnp.int32)
+    for s in range(2):
+        hit = ours & (jnp.broadcast_to(apply_v[pl.ds(s, 1), :], shape) == ranks)
+        key = (2 * ids + s) * n_fsdp + s * half_count + pairs
+        first = jnp.minimum(first, jnp.min(jnp.where(hit, key, none), axis=1, keepdims=True))
+        last = jnp.maximum(last, jnp.max(jnp.where(hit, key, -1), axis=1, keepdims=True))
+    slot_0 = jnp.where(first < none, first & (n_fsdp - 1), n_fsdp)
+    slot_1 = jnp.where(last > first, last & (n_fsdp - 1), n_fsdp)
+    block = jnp.max(jnp.where(ours & (pairs == ranks), ids, 0), axis=1, keepdims=True)
+    owns = jnp.max(jnp.where(ours & (owners == me), 1, 0), axis=1, keepdims=True)
+    lane = lax.broadcasted_iota(jnp.int32, table_v.shape, 1)
+    out = jnp.where(lane == 0, slot_0, slot_1)
+    out = jnp.where(lane == 2, block, out)
+    table_v[...] = jnp.where(lane == 3, owns, out)
 
 
 def local(grad_parts, owner_map, apply_map, gram_old, old_vectors):
@@ -336,21 +365,28 @@
     n_fsdp = lax.axis_size("fsdp")
     per_range = owner_map.shape[0] // n_dp
     stripe, extent = grad_parts.shape[2], grad_parts.shape[3]
-    table = make_table(owner_map, apply_map, n_dp, n_fsdp)
     grads = grad_parts.reshape(n_dp, per_range, stripe, extent)
     far_off = n_dp // 2
     width = extent // N_CHUNK
-    piece = (extent * 2 // n_fsdp, extent // 2)
+    piece = (extent * 2 // n_fsdp, extent // 4)
     vmem, dma = pltpu.VMEM, pltpu.SemaphoreType.DMA
+    in_hbm = [
+        pltpu.with_memory_space_constraint(value, pltpu.HBM)
+        for value in (owner_map[None], apply_map.T, grads, gram_old[0, 0], old_vectors[0, 0])
+    ]
     codes, scales = pl.pallas_call(
         functools.partial(kernel, n_dp, n_fsdp, per_range),
         out_shape=(
             jax.ShapeDtypeStruct((AP_CAP, extent, extent), BF16),
             jax.ShapeDtypeStruct((AP_CAP, extent // QG, extent), BF16),
         ),
-        in_specs=[pl.BlockSpec(memory_space=pltpu.SMEM)] + [pl.BlockSpec(memory_space=pl.ANY)] * 3,
+        in_specs=[pl.BlockSpec(memory_space=pl.ANY)] * 5,
         out_specs=(pl.BlockSpec(memory_space=pltpu.VMEM), pl.BlockSpec(memory_space=pltpu.VMEM)),
         scratch_shapes=[
+            vmem((1, owner_map.shape[0]), jnp.int32),
+            vmem((2, owner_map.shape[0]), jnp.int32),
+            vmem((n_fsdp, 128), jnp.int32),
+            pltpu.SMEM((n_fsdp, 128), jnp.int32),
             vmem((n_dp, per_range, stripe, extent), BF16),
             vmem((far_off, per_range, stripe, extent), BF16),
             vmem((far_off, per_range, stripe, extent), BF16),
@@ -363,22 +399,23 @@
             vmem((extent, extent), BF16),
             vmem((extent, extent), BF16),
             vmem((n_fsdp + 1,) + piece, BF16),
-            vmem((n_fsdp, AP_CAP) + piece, BF16),
-            vmem((n_fsdp, AP_CAP) + piece, BF16),
+            vmem((n_fsdp + 1,) + piece, BF16),
+            vmem((2, n_fsdp, AP_CAP) + piece, BF16),
+            vmem((2, n_fsdp, AP_CAP) + piece, BF16),
             vmem((AP_CAP, extent, 128), F32),
-            dma((3,)),
+            dma((6,)),
             dma((5,)), dma((5,)),
             dma((N_CHUNK, far_off)), dma((N_CHUNK, far_off)),
             dma((N_CHUNK, far_off)), dma((N_CHUNK, far_off)),
             dma, dma((N_CHUNK,)),
-            dma, dma,
-            dma, dma((n_fsdp // 8,)),
+            dma, dma((2,)),
+            dma, dma((2, n_fsdp // 8)),
         ],
         compiler_params=pltpu.CompilerParams(
             collective_id=0, has_side_effects=True, vmem_limit_bytes=48 * 2**20
         ),
         name="refresh",
-    )(table, grads, gram_old[0, 0], old_vectors[0, 0])
+    )(*in_hbm)
     return codes[None, None], jnp.swapaxes(scales, 1, 2)[None, None]
 
 

time: 122 us -> 95.8 us (0.79)
  Pallas kernels: 112 us -> 93.5 us
  local copies, waits for them, and re-layouts: 5.92 us -> 1.58 us
  other arithmetic: 2.72 us -> 0 us
    pallas_call x1, Pallas kernels: 112 us -> 93.5 us  [local(): pl.pallas_call(functools.partial(kernel, n_dp, n_fsdp, per_range), out_sh...]
    unnamed x10 -> x2, local copies, waits for them, and re-layouts: 5.54 us -> 1.58 us
    reduce_or x1 -> x0, other arithmetic: 1.39 us -> none  [make_table(): owns = jnp.any(owners == me).astype(jnp.int32)]
where the time goes in v2:
time: 95.8 us; the launch traced here: 95.7 us
  Pallas kernels  93.5 us (98%)
  local copies, waits for them, and re-layouts  1.58 us (2%)
    pallas_call x1, Pallas kernels, local(): pl.pallas_call(functools.partial(kernel, n_dp, n_fsdp, per_range), out_sh...  93.5 us

profile of v2, /device:TPU:1, one launch (start us, length us, event | category | flops | bytes accessed | tf_op | source)
XLA Modules:
  0.0 95.7 jit_solution(2730105728271248198)
XLA Ops:
  0.6 93.5 %refresh.1 = (bf16[2,512,512]{2,1,0:T(8,128)(2,1)S(1)}, bf16[2,8,512]{2,1,0:T(8,128)(2,1)S(1)}) custom-call(s32[1,224]{1,0:T(1,128)} %bitcast.15, s32[2,224]{1,0:T(2,128)} %bitcast.14, bf16[8,28,8,512]{3,2,1,0:T(8,128)(2,1)} %bitcast.11, bf16[2,512,512]{2,1,0:T(8,128)(2,1)} %bitcast.12, bf16[2,512,512]{2,1,0:T(8,128)(2,1)} %bitcast.13), custom_call_target="tpu_custom_call" | custom-call | tf_op jit(solution)/shard_map/refresh/pallas_call | solution.py:377
  94.1 1.0 %copy.9 = bf16[1,1,2,512,512]{4,3,2,1,0:T(8,128)(2,1)} copy(bf16[1,1,2,512,512]{4,3,2,1,0:T(8,128)(2,1)S(1)} %bitcast.9) | data formatting | bytes 2097152
  95.1 0.6 copy.10

commit v3 on v2

--- a/solution.py
+++ b/solution.py
@@ -167,7 +167,7 @@
         lax.fori_loop(0, half_count, pick, 0)
 
         def post(k, carry):
-            target = me ^ k
+            target = me ^ (n_fsdp - k)
             pltpu.make_async_remote_copy(
                 src_ref=outgoing.at[c, lax.rem(target, half_count)],
                 dst_ref=stripes.at[me, :, columns(c)],
@@ -224,14 +224,15 @@
     state_high, state_low = split(state)
     turned = dot_nn(basis, state_high) + dot_nn(basis, state_low)
     turned = turned / jnp.sqrt(jnp.sum(turned * turned, axis=1, keepdims=True) + norm_eps)
+    row_at = lax.broadcasted_iota(jnp.int32, (extent, extent), 0)
+    col_at = lax.broadcasted_iota(jnp.int32, (extent, extent), 1)
+    identity = jnp.where(row_at == col_at, 1.0, 0.0)
     for _ in range(ITERS - 1):
-        high, low = split(turned)
-        inner_high, inner_low = split(dot_nt(high, high) + dot_nt(high, low) + dot_nt(low, high))
-        turned = 1.5 * turned - 0.5 * (
-            dot_nn(inner_high, high) + dot_nn(inner_high, low) + dot_nn(inner_low, high)
-        )
-    high, low = split(turned)
-    inner_high, inner_low = split(dot_nt(high, high) + dot_nt(high, low) + dot_nt(low, high))
+        high = turned.astype(BF16)
+        gap = (identity - dot_nt(high, high)).astype(BF16)
+        turned = turned + 0.5 * dot_nn(gap, high)
+    high = turned.astype(BF16)
+    gap = (identity - dot_nt(high, high)).astype(BF16)
 
     half_rows = extent // 2
 
@@ -245,15 +246,11 @@
 
     for h in range(2):
         part = slice(h * half_rows, (h + 1) * half_rows)
-        last = 1.5 * turned[:, part] - 0.5 * (
-            dot_nn(inner_high, high[:, part])
-            + dot_nn(inner_high, low[:, part])
-            + dot_nn(inner_low, high[:, part])
-        )
+        last = turned[:, part] + 0.5 * dot_nn(gap, high[:, part])
         iterate_m[pl.ds(h * half_rows, half_rows), :] = last.T.astype(BF16)
 
         def spread(k, carry):
-            target = me ^ k
+            target = me ^ (n_fsdp - k)
             pltpu.make_async_remote_copy(
                 src_ref=iterate_m.at[piece(h, target)], dst_ref=held[h].at[me],
                 send_sem=second_send, recv_sem=second_recv.at[h],
@@ -273,11 +270,12 @@
         wait_bytes(held[h].at[pl.ds(0, n_fsdp - 1)], second_recv.at[h])
 
         def deliver(k, carry):
-            target = me ^ k
+            offset = n_fsdp - k
+            target = me ^ offset
             select(h, target, chosen)
             pltpu.make_async_remote_copy(
                 src_ref=chosen.at[h, target], dst_ref=landed.at[h, me],
-                send_sem=third_send, recv_sem=third_recv.at[h, k // group],
+                send_sem=third_send, recv_sem=third_recv.at[h, offset // group],
                 device_id={"fsdp": target}, device_id_type=MESH,
             ).start()
             return carry
@@ -308,7 +306,7 @@
             scale_m[t, rows, :] = jnp.where(filled, scales, 0.0)
 
     for h in range(2):
-        for g in range(n_fsdp // group):
+        for g in reversed(range(n_fsdp // group)):
             count = group - 1 if g == 0 else group
             wait_bytes(landed.at[h, pl.ds(0, count)], third_recv.at[h, g])
 

time: 95.8 us -> 89.2 us (0.931)
  Pallas kernels: 93.5 us -> 86.7 us
    pallas_call x1, Pallas kernels: 93.5 us -> 86.7 us  [local(): pl.pallas_call(functools.partial(kernel, n_dp, n_fsdp, per_range), out_sh...]
where the time goes in v3:
time: 89.2 us; the launch traced here: 88.9 us
  Pallas kernels  86.7 us (97%)
  local copies, waits for them, and re-layouts  1.58 us (2%)
    pallas_call x1, Pallas kernels, local(): pl.pallas_call(functools.partial(kernel, n_dp, n_fsdp, per_range), out_sh...  86.7 us

profile of v3, /device:TPU:1, one launch (start us, length us, event | category | flops | bytes accessed | tf_op | source)
XLA Modules:
  0.0 88.9 jit_solution(16660185275372718792)
XLA Ops:
  0.6 86.7 %refresh.1 = (bf16[2,512,512]{2,1,0:T(8,128)(2,1)S(1)}, bf16[2,8,512]{2,1,0:T(8,128)(2,1)S(1)}) custom-call(s32[1,224]{1,0:T(1,128)} %bitcast.15, s32[2,224]{1,0:T(2,128)} %bitcast.14, bf16[8,28,8,512]{3,2,1,0:T(8,128)(2,1)} %bitcast.11, bf16[2,512,512]{2,1,0:T(8,128)(2,1)} %bitcast.12, bf16[2,512,512]{2,1,0:T(8,128)(2,1)} %bitcast.13), custom_call_target="tpu_custom_call" | custom-call | tf_op jit(solution)/shard_map/refresh/pallas_call | solution.py:375
  87.3 1.0 %copy.9 = bf16[1,1,2,512,512]{4,3,2,1,0:T(8,128)(2,1)} copy(bf16[1,1,2,512,512]{4,3,2,1,0:T(8,128)(2,1)S(1)} %bitcast.9) | data formatting | bytes 2097152
  88.3 0.6 copy.10

commit v4 on v3

--- a/solution.py
+++ b/solution.py
@@ -16,6 +16,7 @@
 norm_eps = 1e-06
 
 N_CHUNK = 4
+N_STORE = 8
 F32 = jnp.float32
 BF16 = jnp.bfloat16
 
@@ -228,8 +229,9 @@
     col_at = lax.broadcasted_iota(jnp.int32, (extent, extent), 1)
     identity = jnp.where(row_at == col_at, 1.0, 0.0)
     for _ in range(ITERS - 1):
-        high = turned.astype(BF16)
-        gap = (identity - dot_nt(high, high)).astype(BF16)
+        high, low = split(turned)
+        cross = dot_nt(high, low)
+        gap = ((identity - dot_nt(high, high)) - (cross + cross.T)).astype(BF16)
         turned = turned + 0.5 * dot_nn(gap, high)
     high = turned.astype(BF16)
     gap = (identity - dot_nt(high, high)).astype(BF16)
@@ -356,6 +358,19 @@
     out = jnp.where(lane == 0, slot_0, slot_1)
     out = jnp.where(lane == 2, block, out)
     table_v[...] = jnp.where(lane == 3, owns, out)
+
+
+def store(codes, scales, codes_out, scales_out, sems):
+    rows = AP_CAP * codes.shape[1] // N_STORE
+    per_slot = codes.shape[1] // rows
+    copies = [pltpu.make_async_copy(scales, scales_out, sems.at[N_STORE])]
+    for i in range(N_STORE):
+        at = (i // per_slot, pl.ds(i % per_slot * rows, rows))
+        copies.append(pltpu.make_async_copy(codes.at[at], codes_out.at[at], sems.at[i]))
+    for copy in copies:
+        copy.start()
+    for copy in copies:
+        copy.wait()
 
 
 def local(grad_parts, owner_map, apply_map, gram_old, old_vectors):
@@ -414,6 +429,17 @@
         ),
         name="refresh",
     )(*in_hbm)
+    codes, scales = pl.pallas_call(
+        store,
+        out_shape=(
+            jax.ShapeDtypeStruct(codes.shape, BF16), jax.ShapeDtypeStruct(scales.shape, BF16)
+        ),
+        in_specs=[pl.BlockSpec(memory_space=pltpu.VMEM)] * 2,
+        out_specs=[pl.BlockSpec(memory_space=pl.ANY)] * 2,
+        scratch_shapes=[dma((N_STORE + 1,))],
+        compiler_params=pltpu.CompilerParams(vmem_limit_bytes=8 * 2**20),
+        name="store",
+    )(codes, scales)
     return codes[None, None], jnp.swapaxes(scales, 1, 2)[None, None]
 
 

time: 89.2 us -> 88.9 us (level)
  local copies, waits for them, and re-layouts: 1.58 us -> 0 us
  Pallas kernels: 86.7 us -> 88.1 us
    unnamed x2 -> x0, local copies, waits for them, and re-layouts: 1.58 us -> none
    pallas_call x0 -> x1, Pallas kernels: none -> 1.04 us  [local(): pl.pallas_call(store, out_shape=(jax.ShapeDtypeStruct(codes.shape, BF16),...]
where the time goes in v4:
time: 88.9 us; the launch traced here: 88.7 us
  Pallas kernels  88.1 us (99%)
    pallas_call x1, Pallas kernels, local(): pl.pallas_call(functools.partial(kernel, n_dp, n_fsdp, per_range), out_sh...  87.1 us

profile of v4, /device:TPU:1, one launch (start us, length us, event | category | flops | bytes accessed | tf_op | source)
XLA Modules:
  0.0 88.7 jit_solution(8300639873251658627)
XLA Ops:
  0.6 87.1 %refresh.1 = (bf16[2,512,512]{2,1,0:T(8,128)(2,1)S(1)}, bf16[2,8,512]{2,1,0:T(8,128)(2,1)S(1)}) custom-call(s32[1,224]{1,0:T(1,128)} %bitcast.13, s32[2,224]{1,0:T(2,128)} %bitcast.12, bf16[8,28,8,512]{3,2,1,0:T(8,128)(2,1)} %bitcast.9, bf16[2,512,512]{2,1,0:T(8,128)(2,1)} %bitcast.10, bf16[2,512,512]{2,1,0:T(8,128)(2,1)} %bitcast.11), custom_call_target="tpu_custom_call" | custom-call | tf_op jit(solution)/shard_map/refresh/pallas_call | solution.py:390
  87.7 1.0 %store.1 = (bf16[2,512,512]{2,1,0:T(8,128)(2,1)}, bf16[2,8,512]{2,1,0:T(8,128)(2,1)}) custom-call(bf16[2,512,512]{2,1,0:T(8,128)(2,1)S(1)} %get-tuple-element.6.codes, bf16[2,8,512]{2,1,0:T(8,128)(2,1)S(1)} %get-tuple-element.7.scales), custom_call_target="tpu_custom_call" | custom-call | tf_op jit(solution)/shard_map/store/pallas_call | solution.py:432
